TPU v7x, 256 devices: a whole 4x4x8 slice. The times are simulated.
256 devices in a mesh: row: 16 (over z, core), col: 16 (over y, x).
Axes of the slice: x: 4, y: 4, z: 8, core: 2. Of those that a mesh axis runs over, the one named last changes fastest.
Arguments:
- activations: bfloat16 [512, 8192], P('row', 'col'), may hold values from -6 to 6
- out_grads: bfloat16 [512, 29568], P('col', 'row'), may hold values from -6 to 6
- basis_in: bfloat16 [8192, 8192], P('col', 'row'), may hold values from -0.0625 to 0.0625
- basis_out: bfloat16 [29568, 29568], P('row', 'col'), may hold values from -0.03125 to 0.03125
- seq_lengths: int32 [8], replicated, may hold values from 1 to 256, 512 in all
Outputs:
- eigen_diag: float32 [29568, 8192], P('col', 'row')
Inputs may be any that keep to these rules, and one draw needn't show every extreme that they name: `seq_lengths`: the 8 lengths sum to 512 and the longest is exactly 256.
All inputs are finite; a program needn't handle non-finite values.
Results may differ from a plain program's by a relative error of at most 0.0037.
Values may be sent and summed in bfloat16 or wider, within the bound.
A program may use at most 64 MiB of HBM per device.

v0:
```python
import jax
import jax.numpy as jnp
from jax import lax
from jax.sharding import PartitionSpec as P


def local(activations, out_grads, basis_in, basis_out, seq_lengths):
    act_full = lax.all_gather(activations, "row", axis=0, tiled=True)
    act_part = jnp.dot(act_full, basis_in, preferred_element_type=jnp.float32)
    rot_acts = lax.psum(act_part, "col").astype(jnp.bfloat16)
    grad_full = lax.all_gather(out_grads, "col", axis=0, tiled=True)
    grad_part = jnp.dot(grad_full, basis_out, preferred_element_type=jnp.float32)
    rot_grads = lax.psum(grad_part, "row").astype(jnp.bfloat16)
    total_rows = rot_acts.shape[0]
    maxlen = total_rows // 2
    offsets = jnp.cumsum(seq_lengths) - seq_lengths
    acts_pad = jnp.concatenate(
        [rot_acts, jnp.zeros((maxlen, rot_acts.shape[1]), jnp.bfloat16)], axis=0
    )
    grads_pad = jnp.concatenate(
        [rot_grads, jnp.zeros((maxlen, rot_grads.shape[1]), jnp.bfloat16)], axis=0
    )
    total = jnp.zeros((rot_grads.shape[1], rot_acts.shape[1]), jnp.float32)
    for index in range(seq_lengths.shape[0]):
        start = offsets[index]
        keep = (jnp.arange(maxlen) < seq_lengths[index]).astype(jnp.bfloat16)[:, None]
        act_block = lax.dynamic_slice_in_dim(acts_pad, start, maxlen, 0) * keep
        grad_block = lax.dynamic_slice_in_dim(grads_pad, start, maxlen, 0)
        product = lax.dot_general(
            grad_block, act_block, (((0,), (0,)), ((), ())), preferred_element_type=jnp.float32
        )
        total = total + product * product
    return total / total_rows


def solution(mesh):
    in_specs = (P("row", "col"), P("col", "row"), P("col", "row"), P("row", "col"), P())
    out_specs = P("col", "row")
    return jax.shard_map(local, mesh=mesh, in_specs=in_specs, out_specs=out_specs, check_vma=False)
```

profile of v0, /device:TPU:1, one launch (start us, length us, event | category | flops | bytes accessed | tf_op | source)
XLA Modules:
  0.0 233.5 jit_solution(8407644326088578896)
XLA Ops:
  6.5 0.0 copy-start
  6.5 0.0 all-gather.2.cloned.1.call-start
  6.5 0.7 all-gather.2.cloned.1.call-update
  7.3 0.8 reduce-window.9
  8.1 0.7 bitcast_subtract_fusion
  8.7 0.7 fusion.48
  19.5 23.0 %all_gather.7 = bf16[512,512]{1,0:T(8,128)(2,1)S(1)} all-gather(bf16[32,512]{1,0:T(8,128)(2,1)} %param.5), channel_id=1, replica_groups=mesh['row'=16,'col'=16] {'row'}, dimensions={0}, use_global_device_ids=true | all-gather | bytes 557056 | tf_op jit(solution)/shard_map/all_gather | solution.py:8
  42.5 0.0 copy-done
  42.5 0.4 fusion.50
  48.0 1.6 fusion.47
  49.7 0.6 compare_convert_fusion
  50.3 0.6 compare_convert_fusion.2
  51.0 0.6 compare_convert_fusion.3
  51.6 0.6 compare_convert_fusion.4
  52.2 0.6 compare_convert_fusion.5
  52.9 0.7 compare_convert_fusion.6
  53.6 0.5 compare_convert_fusion.7
  54.1 0.7 compare_convert_fusion.1
  54.8 74.8 %all-reduce.4 = bf16[512,512]{1,0:T(8,128)(2,1)S(1)} all-reduce(f32[512,512]{1,0:T(8,128)S(1)} %fusion.50), channel_id=1, replica_groups=mesh['row'=16,'col'=16] {'col'}, use_global_device_ids=true, to_apply=%region_2.0 | all-reduce | flops 262144 | bytes 1572864 | tf_op jit(solution)/shard_map/psum | solution.py:10
  129.6 0.0 all-gather.2.cloned.1.call-done
  129.7 9.6 %fusion.49 = f32[512,1848]{0,1:T(8,128)} fusion(bf16[512,1848]{1,0:T(8,128)(2,1)} %all-gather.2.cloned.1.call-done, bf16[1848,1848]{1,0:T(8,128)(2,1)} %param.8), kind=kOutput, calls=%fused_computation.67 | convolution fusion | flops 3497066496 | bytes 12507264 | tf_op jit(solution)/shard_map/dot_general | solution.py:12
  139.3 71.8 %all-reduce.5 = bf16[512,1848]{0,1:T(8,128)(2,1)S(1)} all-reduce(f32[512,1848]{0,1:T(8,128)} %fusion.49), channel_id=1, replica_groups=mesh['row'=16,'col'=16] {'row'}, use_global_device_ids=true, to_apply=%region_0.0 | all-reduce | flops 946176 | bytes 5677056 | tf_op jit(solution)/shard_map/psum | solution.py:13
  211.1 0.8 fusion.2
  211.9 0.8 fusion.3
  212.7 0.8 fusion.4
  213.5 0.8 fusion.5
  214.3 0.8 fusion.6
  215.1 2.6 %fusion = f32[1848,512]{1,0:T(8,128)} fusion(s32[]{:T(128)S(6)} %select_n.32, bf16[512,1848]{0,1:T(8,128)(2,1)S(1)} %all-reduce.5, bf16[512,512]{1,0:T(8,128)(2,1)S(1)} %all-reduce.4, bf16[256]{0:T(256)(128)(2,1)S(1)} %compare_convert_fusion.7), kind=kOutput, calls=%fused_computation.17 | convolution fusion | flops 484966400 | bytes 6202880 | tf_op jit(solution)/shard_map/dot_general | solution.py:29
  217.7 2.7 %fusion.1 = f32[1848,512]{1,0:T(8,128)} fusion(s32[]{:T(128)S(6)} %select_n.33, bf16[512,1848]{0,1:T(8,128)(2,1)S(1)} %all-reduce.5, bf16[512,512]{1,0:T(8,128)(2,1)S(1)} %all-reduce.4, bf16[256]{0:T(256)(128)(2,1)S(1)} %compare_convert_fusion.6), kind=kOutput, calls=%fused_computation.18 | convolution fusion | flops 484966400 | bytes 6202880 | tf_op jit(solution)/shard_map/dot_general | solution.py:29
  220.4 6.2 %add_multiply_fusion = f32[1848,512]{1,0:T(8,128)} fusion(f32[1848,512]{1,0:T(8,128)S(1)} %fusion.6, f32[1848,512]{1,0:T(8,128)S(1)} %fusion.5, f32[1848,512]{1,0:T(8,128)S(1)} %fusion.4, f32[1848,512]{1,0:T(8,128)S(1)} %fusion.3, f32[1848,512]{1,0:T(8,128)S(1)} %fusion.2, f32[1848,512]{1,0:T(8,128)} %fusion.1, f32[1848,512]{1,0:T(8,128)} %fusion, ...), kind=kOutput, calls=%fused_computation.8 | convolution fusion | flops 500105216 | bytes 32695808 | tf_op jit(solution)/shard_map/dot_general | solution.py:29
Async XLA Ops:
  6.5 36.0 %copy-start = (bf16[512,512]{1,0:T(8,128)(2,1)S(1)}, bf16[512,512]{1,0:T(8,128)(2,1)}, u32[]{:S(2)}) copy-start(bf16[512,512]{1,0:T(8,128)(2,1)} %param.7) | copy-start | bytes 1572868
  6.5 123.1 %all-gather.2.cloned.1.call-start = ((), (), s32[]{:S(2)}) async-start(), calls=%async_computation | async-start | bytes 2088960 | tf_op jit(solution)/shard_map/all_gather | solution.py:11
Sparse Core Ops, SparseCore 0:
  9.8 53.1 all-gather.1
where the time goes:
time: 234 us; the launch traced here: 233 us
  blocking collectives  170 us (73%)
  between operations  28.7 us (12%)
  matrix products  25.6 us (11%)
  other arithmetic  6.57 us (3%)
    psum x1, blocking collectives, local(): rot_acts = lax.psum(act_part, 'col').astype(jnp.bfloat16)  74.8 us
    psum x1, blocking collectives, local(): rot_grads = lax.psum(grad_part, 'row').astype(jnp.bfloat16)  71.8 us
    all_gather x1, blocking collectives, local(): act_full = lax.all_gather(activations, 'row', axis=0, tiled=True)  23 us
    dot_general x8, matrix products, local(): lax.dot_general(grad_block, act_block, (((0,), (0,)), ((), ())), preferre...  15.5 us
    dot_general x1, matrix products, local(): jnp.dot(grad_full, basis_out, preferred_element_type=jnp.float32)  9.62 us
    convert_element_type x8, other arithmetic, local(): (jnp.arange(maxlen) < seq_lengths[index]).astype(jnp.bfloat16)[:, None]  5.08 us
  transfers between devices with their start and end apart: 1, of which 0 were waited for; matrix products, arithmetic and copies ran while one was open for 4% of the time, Pallas kernels for 0%

commit v1 on v0

v1 whole, which is shorter than its diff:
```python
import functools

import jax
import jax.numpy as jnp
from jax import lax
from jax.experimental import pallas as pl
from jax.experimental.pallas import tpu as pltpu
from jax.sharding import PartitionSpec as P

MESH = pl.DeviceIdType.MESH
F32, BF16 = jnp.float32, jnp.bfloat16
NZ, NY, NX = 8, 4, 4
PLUS, MINUS = 0, 1


def comm_kernel(act, grad, basis_in, basis_out, rg_out, ra_out,
                gbuf, bo, part, psend, sib, rsend, rrecv, rg,
                abuf, bi, apart, arecv, ra,
                lsem, g_send, g_recv, sib_send, sib_recv, rs_send, rs_recv,
                ag_send, ag_recv, agx_send, agx_recv,
                az_send, az_recv, ax_send, ax_recv, ar_send, ar_recv, aa_send, aa_recv):
    row, col = lax.axis_index("row"), lax.axis_index("col")
    z, k = row // 2, row % 2
    y, x = col // 4, col % 4

    def dev(z=z, k=k, y=y, x=x):
        return {"row": z * 2 + k, "col": y * 4 + x}

    def zrel(d):
        return (z + (d + NZ)) % NZ

    def xyrel(dy, dx):
        return (y + dy + NY) % NY, (x + dx + NX) % NX

    pending = []

    def remote(src, dst, ssem, rsem, to):
        copy = pltpu.make_async_remote_copy(
            src_ref=src, dst_ref=dst, send_sem=ssem, recv_sem=rsem,
            device_id=to, device_id_type=MESH)
        copy.start()
        pending.append(copy)

    def arrived(dst, ssem, rsem):
        pltpu.make_async_remote_copy(
            src_ref=dst, dst_ref=dst, send_sem=ssem, recv_sem=rsem,
            device_id=dev(), device_id_type=MESH).wait_recv()

    loads = {}
    for index, (name, src, dst) in enumerate((
            ("ga", grad.at[pl.ds(0, 16)], gbuf.at[0, pl.ds(0, 16)]),
            ("gb", grad.at[pl.ds(16, 16)], gbuf.at[0, pl.ds(64, 16)]),
            ("act", act, abuf.at[row]),
            ("bi", basis_in, bi),
            ("bo", basis_out, bo))):
        loads[name] = pltpu.make_async_copy(src, dst, lsem.at[index])
        loads[name].start()

    peers = [dev(z=zrel(d)) for d in range(1, NZ)]
    peers += [dev(k=1 - k)]
    for i in range(1, 16):
        py, px = xyrel(i // 4, i % 4)
        peers.append(dev(y=py, x=px))
    barrier = pltpu.get_barrier_semaphore()
    for peer in peers:
        pl.semaphore_signal(barrier, inc=1, device_id=peer, device_id_type=MESH)
    pl.semaphore_wait(barrier, len(peers))

    def gslot(e, j):
        return gbuf.at[e, pl.ds(16 * j, 16)]

    counter = [0]

    def gsend(src, e, j, to):
        remote(src, gslot(e, j), g_send.at[counter[0]], g_recv.at[e, j], to)
        counter[0] += 1

    def garrived(e, j):
        arrived(gslot(e, j), g_send.at[0], g_recv.at[e, j])

    def xy(dy, dx):
        py, px = xyrel(dy, dx)
        return dev(y=py, x=px)

    loads["ga"].wait()
    loads["gb"].wait()
    for d in (1, 3, 2):
        gsend(gslot(0, 0), 0, d, xy(0, -d))
        gsend(gslot(0, 4), 0, 4 + d, xy(-d, 0))
    gsend(gslot(0, 0), 1, 0, xy(-1, 0))
    gsend(gslot(0, 0), 3, 0, xy(1, 0))
    gsend(gslot(0, 4), 1, 4, xy(0, -1))
    gsend(gslot(0, 4), 3, 4, xy(0, 1))

    loads["act"].wait()
    for i, d in enumerate((1, 7, 2, 6, 3, 5, 4)):
        remote(abuf.at[row], abuf.at[row], az_send.at[d], az_recv.at[d], dev(z=zrel(-d)))
    remote(abuf.at[row], abuf.at[row], ax_send.at[0], ax_recv.at[0], dev(k=1 - k))

    for d in (1, 3, 2):
        garrived(0, d)
        gsend(gslot(0, d), 1, d, xy(-1, 0))
        gsend(gslot(0, d), 3, d, xy(1, 0))
        garrived(0, 4 + d)
        gsend(gslot(0, 4 + d), 1, 4 + d, xy(0, -1))
        gsend(gslot(0, 4 + d), 3, 4 + d, xy(0, 1))

    def far(e, j):
        garrived(e, j)
        step = -1 if e == 1 else 1
        gsend(gslot(e, j), 2, j, xy(step, 0) if j < 4 else xy(0, step))

    far(1, 0)
    far(1, 4)

    def product(e, m):
        for lo, hi in ((0, 512), (512, 1024), (1024, 1536), (1536, 1848)):
            value = jnp.dot(gbuf[e], bo[:, lo:hi], preferred_element_type=F32)
            if m != 1:
                part[m, :, lo:hi] = value
            if m != 2:
                psend[m, :, lo:hi] = value.astype(BF16)

    loads["bo"].wait()
    product(0, 0)

    sibling = dev(k=1 - k)

    def give(m, slot):
        remote(psend.at[m], sib.at[slot], sib_send.at[slot], sib_recv.at[slot], sibling)

    def give_when(which, m, slot):
        @pl.when(k == which)
        def _():
            pltpu.make_async_remote_copy(
                src_ref=psend.at[m], dst_ref=sib.at[slot], send_sem=sib_send.at[slot],
                recv_sem=sib_recv.at[slot], device_id=sibling, device_id_type=MESH).start()

    give_when(1, 0, 0)

    def chunk_of(slot):
        return jnp.where(k == 0, 0, 2) if slot == 0 else jnp.where(k == 0, 1, 3)

    def part_of(slot):
        return jnp.where(k == 0, 0, 3) if slot == 0 else 2

    def own(slot, j):
        at = pl.ds(pl.multiple_of(16 * j, 16), 16)
        return part[part_of(slot), at, :] + sib[slot, at, :].astype(F32)

    def long_way(slot):
        return PLUS if slot == 0 else MINUS

    def rs_hop(slot, way, hop):
        sign = 1 if way == PLUS else -1
        first = 0 if way == long_way(slot) else 1
        if hop < first:
            return
        value = own(slot, zrel(sign * (4 - hop)))
        if hop > first:
            arrived(rrecv.at[slot, way, hop - 1], rs_send.at[slot, way, hop - 1], rs_recv.at[slot, way, hop - 1])
            value = value + rrecv[slot, way, hop - 1].astype(F32)
        rsend[slot, way, hop] = value.astype(BF16)
        remote(rsend.at[slot, way, hop], rrecv.at[slot, way, hop],
               rs_send.at[slot, way, hop], rs_recv.at[slot, way, hop], dev(z=zrel(sign)))

    def block_of(slot, j):
        e = chunk_of(slot)
        first = 2 * (((y + e) % 4) * 4 + (x + j) % 4)
        second = 2 * (((y + j) % 4) * 4 + (x + e) % 4) + 1
        return jnp.where(j < 4, first, second)

    def rs_end(slot):
        value = own(slot, z)
        for way in (PLUS, MINUS):
            arrived(rrecv.at[slot, way, 3], rs_send.at[slot, way, 3], rs_recv.at[slot, way, 3])
            value = value + rrecv[slot, way, 3].astype(F32)
        rg[block_of(slot, z)] = value.astype(BF16)

    def to_sibling(slot, d):
        at = rg.at[block_of(slot, zrel(d))]
        remote(at, at, agx_send.at[slot, d % NZ], agx_recv.at[slot, d % NZ], sibling)

    def from_sibling(slot, d):
        e = jnp.where(k == 0, 2, 0) if slot == 0 else jnp.where(k == 0, 3, 1)
        j = zrel(d)
        first = 2 * (((y + e) % 4) * 4 + (x + j) % 4)
        second = 2 * (((y + j) % 4) * 4 + (x + e) % 4) + 1
        at = rg.at[jnp.where(j < 4, first, second)]
        arrived(at, agx_send.at[slot, d % NZ], agx_recv.at[slot, d % NZ])

    def ag_hop(slot, way, hop):
        sign = 1 if way == PLUS else -1
        last = 4 if way == long_way(slot) else 3
        if hop > last:
            return
        at = rg.at[block_of(slot, zrel(-sign * hop))]
        if hop > 0:
            arrived(at, ag_send.at[slot, way, hop - 1], ag_recv.at[slot, way, hop - 1])
        if hop < last:
            remote(at, at, ag_send.at[slot, way, hop], ag_recv.at[slot, way, hop], dev(z=zrel(sign)))
        if hop > 0:
            to_sibling(slot, -sign * hop)

    def ag_both(slot, hop):
        ag_hop(slot, PLUS, hop)
        ag_hop(slot, MINUS, hop)
        if hop == 0:
            to_sibling(slot, 0)

    def rs_both(slot, hop):
        rs_hop(slot, PLUS, hop)
        rs_hop(slot, MINUS, hop)

    for j in (1, 5):
        far(1, j)
    for j in (2, 3, 6, 7):
        far(3, j)
    for j in (2, 3, 6, 7):
        garrived(1, j)
    for j in (0, 1, 4, 5):
        garrived(3, j)

    for d in range(1, NZ):
        r = zrel(d) * 2 + k
        arrived(abuf.at[r], az_send.at[d], az_recv.at[d])
        remote(abuf.at[r], abuf.at[r], ax_send.at[d], ax_recv.at[d], sibling)

    product(jnp.where(k == 0, 3, 1), 1)
    give(1, 1)
    product(jnp.where(k == 0, 1, 3), 2)
    arrived(sib.at[1], sib_send.at[1], sib_recv.at[1])
    rs_both(1, 0)
    for j in range(8):
        garrived(2, j)
    product(2, 3)
    give_when(0, 3, 0)
    rs_both(1, 1)
    arrived(sib.at[0], sib_send.at[0], sib_recv.at[0])
    rs_both(0, 0)

    loads["bi"].wait()
    for d in range(NZ):
        arrived(abuf.at[zrel(d) * 2 + 1 - k], ax_send.at[d], ax_recv.at[d])
    for lo in range(0, 16, 4):
        value = jnp.dot(abuf[lo:lo + 4].reshape(128, 512), bi[...], preferred_element_type=F32)
        apart[lo:lo + 4] = value.reshape(4, 32, 512)
    for i in range(1, 16):
        py, px = xyrel(-(i // 4), -(i % 4))
        remote(apart.at[py * 4 + px], arecv.at[i], ar_send.at[i], ar_recv.at[i], dev(y=py, x=px))

    rs_both(1, 2)
    rs_both(0, 1)
    rs_both(1, 3)
    rs_both(0, 2)
    rs_end(1)
    ag_both(1, 0)
    rs_both(0, 3)
    ag_both(1, 1)
    rs_end(0)
    ag_both(0, 0)
    ag_both(1, 2)

    value = apart[col]
    for i in range(1, 16):
        arrived(arecv.at[i], ar_send.at[i], ar_recv.at[i])
        value = value + arecv[i]
    ra[col] = value.astype(BF16)
    for i in range(1, 16):
        py, px = xyrel(-(i // 4), -(i % 4))
        remote(ra.at[col], ra.at[col], aa_send.at[i], aa_recv.at[i], dev(y=py, x=px))

    ag_both(0, 1)
    ag_both(1, 3)
    ag_both(0, 2)
    ag_both(1, 4)
    ag_both(0, 3)
    ag_both(0, 4)

    for i in range(1, 16):
        py, px = xyrel(i // 4, i % 4)
        arrived(ra.at[py * 4 + px], aa_send.at[i], aa_recv.at[i])
    ra_copy = pltpu.make_async_copy(ra, ra_out, lsem.at[0])
    ra_copy.start()
    for slot in (1, 0):
        for d in (0, 1, 7, 2, 6, 3, 5, 4):
            from_sibling(slot, d)
    rg_copy = pltpu.make_async_copy(rg, rg_out, lsem.at[1])
    rg_copy.start()
    for copy in pending:
        copy.wait_send()
    pltpu.make_async_remote_copy(
        src_ref=psend.at[0], dst_ref=sib.at[0], send_sem=sib_send.at[0],
        recv_sem=sib_recv.at[0], device_id=sibling, device_id_type=MESH).wait_send()
    ra_copy.wait()
    rg_copy.wait()


def gathered(activations, out_grads, basis_in, basis_out):
    ff, d = basis_out.shape[1], basis_in.shape[1]
    vmem, dma = pltpu.VMEM, pltpu.SemaphoreType.DMA
    any_ = pl.BlockSpec(memory_space=pl.ANY)
    return pl.pallas_call(
        comm_kernel,
        out_shape=(jax.ShapeDtypeStruct((32, 16, ff), BF16), jax.ShapeDtypeStruct((16, 32, d), BF16)),
        in_specs=[any_] * 4,
        out_specs=(any_, any_),
        scratch_shapes=[
            vmem((4, 128, ff), BF16), vmem((ff, ff), BF16), vmem((4, 128, ff), F32),
            vmem((4, 128, ff), BF16), vmem((2, 128, ff), BF16),
            vmem((2, 2, 4, 16, ff), BF16), vmem((2, 2, 4, 16, ff), BF16), vmem((32, 16, ff), BF16),
            vmem((16, 32, d), BF16), vmem((d, d), BF16), vmem((16, 32, d), F32), vmem((16, 32, d), F32),
            vmem((16, 32, d), BF16),
            dma((5,)), dma((30,)), dma((4, 8)), dma((2,)), dma((2,)), dma((2, 2, 4)), dma((2, 2, 4)),
            dma((2, 2, 4)), dma((2, 2, 4)), dma((2, 8)), dma((2, 8)),
            dma((8,)), dma((8,)), dma((8,)), dma((8,)), dma((16,)), dma((16,)), dma((16,)), dma((16,)),
        ],
        compiler_params=pltpu.CompilerParams(
            collective_id=0, has_side_effects=True, vmem_limit_bytes=56 << 20),
        name="gather_rotate",
    )(activations, out_grads, basis_in, basis_out)


TILE = 384


def diag_kernel(bounds, rg, ra, out, gt):
    gt[...] = rg[...].T
    out[...] = jnp.zeros_like(out)

    def one(s, carry):
        start, end = bounds[s], bounds[s + 1]

        def window(w):
            base = pl.multiple_of(w * 256, 256)
            token = base + lax.broadcasted_iota(jnp.int32, (256, 1), 0)
            keep = (token >= start) & (token < end)
            block = ra[pl.ds(base, 256), :]
            block = jnp.where(keep, block, jnp.zeros_like(block))
            return jnp.dot(gt[:, pl.ds(base, 256)], block, preferred_element_type=F32)

        both = (start < 256) & (end > 256)

        @pl.when(jnp.logical_not(both))
        def _():
            p = window(jnp.where(start < 256, 0, 1))
            out[...] += p * p

        @pl.when(both)
        def _():
            p = window(0) + window(1)
            out[...] += p * p

        return carry

    lax.fori_loop(0, 8, one, 0)
    out[...] = out[...] * (1.0 / 512.0)


def diagonal(bounds, rg, ra):
    tokens, ff = rg.shape
    d = ra.shape[1]
    return pl.pallas_call(
        diag_kernel,
        out_shape=jax.ShapeDtypeStruct((ff, d), F32),
        grid_spec=pltpu.PrefetchScalarGridSpec(
            num_scalar_prefetch=1,
            grid=(pl.cdiv(ff, TILE),),
            in_specs=[
                pl.BlockSpec((tokens, TILE), lambda i, b: (0, i)),
                pl.BlockSpec((tokens, d), lambda i, b: (0, 0)),
            ],
            out_specs=pl.BlockSpec((TILE, d), lambda i, b: (i, 0)),
            scratch_shapes=[pltpu.VMEM((TILE, tokens), BF16)],
        ),
        compiler_params=pltpu.CompilerParams(vmem_limit_bytes=40 << 20),
        name="eigen_diagonal",
    )(bounds, rg, ra)


def local(activations, out_grads, basis_in, basis_out, seq_lengths):
    rg, ra = gathered(activations, out_grads, basis_in, basis_out)
    bounds = jnp.concatenate([jnp.zeros((1,), jnp.int32), jnp.cumsum(seq_lengths)]).astype(jnp.int32)
    rg = rg.reshape(512, rg.shape[-1])
    ra = ra.reshape(512, ra.shape[-1])
    return diagonal(bounds, rg, ra)


def solution(mesh):
    in_specs = (P("row", "col"), P("col", "row"), P("col", "row"), P("row", "col"), P())
    out_specs = P("col", "row")
    return jax.shard_map(local, mesh=mesh, in_specs=in_specs, out_specs=out_specs, check_vma=False)
```

time: 234 us -> 81.8 us (0.35)
  blocking collectives: 170 us -> 0 us
  Pallas kernels: 0 us -> 78.1 us
  between operations: 28.7 us -> 0.02 us
  matrix products: 25.6 us -> 0 us
  other arithmetic: 6.57 us -> 0.91 us
    psum x2 -> x0, blocking collectives: 147 us -> none  [the longest x1 74.8 us: local(): rot_acts = lax.psum(act_part, 'col').astype(jnp.bfloat16)]
    pallas_call x0 -> x2, Pallas kernels: none -> 78.1 us  [the longest x1 63.2 us: gathered(): pl.pallas_call(comm_kernel, out_shape=(jax.ShapeDtypeStruct((32, 16, ff),...]
    dot_general x10 -> x0, matrix products: 25.6 us -> none  [the longest x8 15.5 us: local(): lax.dot_general(grad_block, act_block, (((0,), (0,)), ((), ())), preferre...]
    all_gather x1 -> x0, blocking collectives: 23 us -> none  [local(): act_full = lax.all_gather(activations, 'row', axis=0, tiled=True)]
    convert_element_type x8 -> x0, other arithmetic: 5.08 us -> none  [local(): (jnp.arange(maxlen) < seq_lengths[index]).astype(jnp.bfloat16)[:, None]]
    unnamed x2 -> x4, local copies, waits for them, and re-layouts: 0.01 us -> 2.58 us
  transfers between devices with their start and end apart: 1 -> 0, of which waited for: 0 -> 0; matrix products, arithmetic and copies ran while one was open for 4% -> 0% of each run, Pallas kernels for 0% -> 0%
where the time goes in v1:
time: 81.8 us; the launch traced here: 81.6 us
  Pallas kernels  78.1 us (95%)
  local copies, waits for them, and re-layouts  2.58 us (3%)
  other arithmetic  0.91 us (1%)
    pallas_call x1, Pallas kernels, gathered(): pl.pallas_call(comm_kernel, out_shape=(jax.ShapeDtypeStruct((32, 16, ff),...  63.2 us
    pallas_call x1, Pallas kernels, diagonal(): pl.pallas_call(diag_kernel, out_shape=jax.ShapeDtypeStruct((ff, d), F32),...  14.9 us
    unnamed x4, local copies, waits for them, and re-layouts  2.58 us

profile of v1, /device:TPU:1, one launch (start us, length us, event | category | flops | bytes accessed | tf_op | source)
XLA Modules:
  0.0 81.6 jit_solution(3936880312926729214)
XLA Ops:
  0.0 0.8 %reduce-window.9 = s32[8,1]{0,1:T(1,128)S(1)} reduce-window(s32[8,1]{0,1:T(1,128)} %bitcast.6, s32[]{:T(128)} %constant.5.clone.1), window={size=8x1 pad=7_0x0_0}, to_apply=%region_0.0 | reduce-window | flops 56 | bytes 68 | tf_op jit(solution)/shard_map/reduce-window.4
  0.8 0.1 pad_add_fusion.bounds
  0.9 63.2 %gather_rotate.1 = (bf16[32,16,1848]{2,1,0:T(8,128)(2,1)}, bf16[16,32,512]{2,1,0:T(8,128)(2,1)}) custom-call(bf16[32,512]{1,0:T(8,128)(2,1)} %act.1, bf16[32,1848]{1,0:T(8,128)(2,1)} %grad.1, bf16[512,512]{1,0:T(8,128)(2,1)} %basis_in.1, bf16[1848,1848]{1,0:T(8,128)(2,1)} %basis_out.1), custom_call_target="tpu_custom_call" | custom-call | tf_op jit(solution)/shard_map/gather_rotate/pallas_call | solution.py:303
  64.1 0.0 copy-start
  64.2 1.5 %copy-done = bf16[32,16,1848]{2,1,0:T(8,128)(2,1)S(1)} copy-done((bf16[32,16,1848]{2,1,0:T(8,128)(2,1)S(1)}, bf16[32,16,1848]{2,1,0:T(8,128)(2,1)}, u32[]{:S(2)}) %copy-start) | copy-done | bytes 1892376
  65.7 0.0 copy-start.1
  65.7 1.0 %copy-done.1 = bf16[16,32,512]{2,1,0:T(8,128)(2,1)S(1)} copy-done((bf16[16,32,512]{2,1,0:T(8,128)(2,1)S(1)}, bf16[16,32,512]{2,1,0:T(8,128)(2,1)}, u32[]{:S(2)}) %copy-start.1) | copy-done | bytes 524312
  66.7 14.9 %eigen_diagonal.1 = f32[1848,512]{1,0:T(8,128)} custom-call(s32[9]{0:T(128)S(1)} %pad_add_fusion.bounds, bf16[512,1848]{1,0:T(8,128)(2,1)S(1)} %bitcast.4, bf16[512,512]{1,0:T(8,128)(2,1)S(1)} %bitcast.5), custom_call_target="tpu_custom_call" | custom-call | tf_op jit(solution)/shard_map/eigen_diagonal/pallas_call | solution.py:363
Async XLA Ops:
  64.1 1.5 %copy-start = (bf16[32,16,1848]{2,1,0:T(8,128)(2,1)S(1)}, bf16[32,16,1848]{2,1,0:T(8,128)(2,1)}, u32[]{:S(2)}) copy-start(bf16[32,16,1848]{2,1,0:T(8,128)(2,1)} %get-tuple-element.7) | copy-start | bytes 5677060
  65.7 1.0 %copy-start.1 = (bf16[16,32,512]{2,1,0:T(8,128)(2,1)S(1)}, bf16[16,32,512]{2,1,0:T(8,128)(2,1)}, u32[]{:S(2)}) copy-start(bf16[16,32,512]{2,1,0:T(8,128)(2,1)} %get-tuple-element.8) | copy-start | bytes 1572868

commit v2 on v0

v2 whole, which is shorter than its diff:
```python
import jax
import jax.numpy as jnp
from jax import lax
from jax.experimental import pallas as pl
from jax.experimental.pallas import tpu as pltpu
from jax.sharding import PartitionSpec as P

MESH = pl.DeviceIdType.MESH
F32, BF16 = jnp.float32, jnp.bfloat16
NZ, NY, NX = 8, 4, 4
PLUS, MINUS = 0, 1


def comm_kernel(act, grad, basis_in, basis_out, rg, ra,
                gbuf, bo, part, psend, sib, rsend, rrecv,
                abuf, bi, apart, arecv,
                lsem, g_send, g_recv, sib_send, sib_recv, rs_send, rs_recv,
                ag_send, ag_recv, agx_send, agx_recv,
                az_send, az_recv, ax_send, ax_recv, ar_send, ar_recv, aa_send, aa_recv):
    row, col = lax.axis_index("row"), lax.axis_index("col")
    z, k = row // 2, row % 2
    y, x = col // 4, col % 4

    def dev(z=z, k=k, y=y, x=x):
        return {"row": z * 2 + k, "col": y * 4 + x}

    def zrel(d):
        return (z + (d + NZ)) % NZ

    def xyrel(dy, dx):
        return (y + dy + NY) % NY, (x + dx + NX) % NX

    def remote(src, dst, ssem, rsem, to):
        pltpu.make_async_remote_copy(
            src_ref=src, dst_ref=dst, send_sem=ssem, recv_sem=rsem,
            device_id=to, device_id_type=MESH).start()

    def arrived(dst, ssem, rsem):
        pltpu.make_async_remote_copy(
            src_ref=dst, dst_ref=dst, send_sem=ssem, recv_sem=rsem,
            device_id=dev(), device_id_type=MESH).wait_recv()

    def sent(src, ssem, rsem):
        pltpu.make_async_remote_copy(
            src_ref=src, dst_ref=src, send_sem=ssem, recv_sem=rsem,
            device_id=dev(), device_id_type=MESH).wait_send()

    inner, outer = k == 0, k == 1

    peers = [dev(z=zrel(d)) for d in range(1, NZ)]
    peers += [dev(k=1 - k)]
    for i in range(1, 16):
        py, px = xyrel(i // 4, i % 4)
        peers.append(dev(y=py, x=px))
    barrier = pltpu.get_barrier_semaphore()
    for peer in peers:
        pl.semaphore_signal(barrier, inc=1, device_id=peer, device_id_type=MESH)
    loads = {}
    for index, (name, src, dst) in enumerate((
            ("ga", grad.at[pl.ds(0, 16)], gbuf.at[0, pl.ds(0, 16)]),
            ("gb", grad.at[pl.ds(16, 16)], gbuf.at[0, pl.ds(64, 16)]),
            ("act", act, abuf.at[row]),
            ("bi", basis_in, bi),
            ("bo", basis_out, bo))):
        loads[name] = pltpu.make_async_copy(src, dst, lsem.at[index])
        loads[name].start()

    pl.semaphore_wait(barrier, len(peers))

    def gslot(e, j):
        return gbuf.at[e, pl.ds(16 * j, 16)]

    counter = [0]

    def gsend(src, e, j, to):
        remote(src, gslot(e, j), g_send.at[counter[0]], g_recv.at[e, j], to)
        counter[0] += 1

    def gsent():
        for i in range(30):
            sent(gslot(0, 0), g_send.at[i], g_recv.at[0, 0])

    def garrived(e, j):
        arrived(gslot(e, j), g_send.at[0], g_recv.at[e, j])

    def xy(dy, dx):
        py, px = xyrel(dy, dx)
        return dev(y=py, x=px)

    loads["ga"].wait()
    loads["gb"].wait()
    for d in (1, 3, 2):
        gsend(gslot(0, 0), 0, d, xy(0, -d))
        gsend(gslot(0, 4), 0, 4 + d, xy(-d, 0))
    gsend(gslot(0, 0), 1, 0, xy(-1, 0))
    gsend(gslot(0, 0), 3, 0, xy(1, 0))
    gsend(gslot(0, 4), 1, 4, xy(0, -1))
    gsend(gslot(0, 4), 3, 4, xy(0, 1))

    loads["act"].wait()
    for i, d in enumerate((1, 7, 2, 6, 3, 5, 4)):
        remote(abuf.at[row], abuf.at[row], az_send.at[d], az_recv.at[d], dev(z=zrel(-d)))
    remote(abuf.at[row], abuf.at[row], ax_send.at[0], ax_recv.at[0], dev(k=1 - k))

    for d in (1, 3, 2):
        garrived(0, d)
        gsend(gslot(0, d), 1, d, xy(-1, 0))
        gsend(gslot(0, d), 3, d, xy(1, 0))
        garrived(0, 4 + d)
        gsend(gslot(0, 4 + d), 1, 4 + d, xy(0, -1))
        gsend(gslot(0, 4 + d), 3, 4 + d, xy(0, 1))

    def far(e, j):
        garrived(e, j)
        step = -1 if e == 1 else 1
        gsend(gslot(e, j), 2, j, xy(step, 0) if j < 4 else xy(0, step))

    far(1, 0)
    far(1, 4)

    sibling = dev(k=1 - k)

    def product(e):
        for lo, hi in ((0, 512), (512, 1024), (1024, 1536), (1536, 1848)):
            value = jnp.dot(gbuf[e], bo[:, lo:hi], preferred_element_type=F32)

            @pl.when(inner)
            def _():
                psend[e, :, lo:hi] = value.astype(BF16)

            @pl.when(outer)
            def _():
                part[e, :, lo:hi] = value

        @pl.when(inner)
        def _():
            remote(psend.at[e], sib.at[e], sib_send.at[e], sib_recv.at[e], sibling)

    def own(e, j):
        at = pl.ds(pl.multiple_of(16 * j, 16), 16)
        return part[e, at, :] + sib[e, at, :].astype(F32)

    def long_way(e):
        return PLUS if e < 2 else MINUS

    def rs_send_own(e, way, index, to_owner, to):
        sign = 1 if way == PLUS else -1
        rsend[e, way, index] = own(e, zrel(sign * to_owner)).astype(BF16)
        remote(rsend.at[e, way, index], rrecv.at[e, way, index],
               rs_send.at[e, way, index], rs_recv.at[e, way, index], dev(z=zrel(sign * to)))

    def rs_take(e, way, index):
        arrived(rrecv.at[e, way, index], rs_send.at[e, way, index], rs_recv.at[e, way, index])
        return rrecv[e, way, index].astype(F32)

    def rs_start(e):
        rs_send_own(e, long_way(e), 1, 4, 2)
        for way in (long_way(e), 1 - long_way(e)):
            rs_send_own(e, way, 0, 3, 1)
        for way in (long_way(e), 1 - long_way(e)):
            rs_send_own(e, way, 2, 1, 1)

    def rs_relay(e):
        for way in (long_way(e), 1 - long_way(e)):
            sign = 1 if way == PLUS else -1
            value = own(e, zrel(sign * 2)) + rs_take(e, way, 0)
            if way == long_way(e):
                value = value + rs_take(e, way, 1)
            rsend[e, way, 3] = value.astype(BF16)
            remote(rsend.at[e, way, 3], rrecv.at[e, way, 3],
                   rs_send.at[e, way, 3], rs_recv.at[e, way, 3], dev(z=zrel(sign * 2)))

    def block_of(e, j):
        first = 2 * (((y + e) % 4) * 4 + (x + j) % 4)
        second = 2 * (((y + j) % 4) * 4 + (x + e) % 4) + 1
        return jnp.where(j < 4, first, second)

    def rs_end(e):
        value = own(e, z)
        for index in (2, 3):
            for way in (PLUS, MINUS):
                value = value + rs_take(e, way, index)
        rg[block_of(e, z)] = value.astype(BF16)

    def over(e, d):
        at = rg.at[block_of(e, zrel(d))]
        remote(at, at, agx_send.at[e, d % NZ], agx_recv.at[e, d % NZ], sibling)

    def ag_hop(e, way, hop):
        sign = 1 if way == PLUS else -1
        last = 4 if way == long_way(e) else 3
        if hop > last:
            return
        at = rg.at[block_of(e, zrel(-sign * hop))]
        if hop > 0:
            arrived(at, ag_send.at[e, way, hop - 1], ag_recv.at[e, way, hop - 1])
        if hop < last:
            remote(at, at, ag_send.at[e, way, hop], ag_recv.at[e, way, hop], dev(z=zrel(sign)))

    def ag_over(e, way, hop):
        if hop <= (4 if way == long_way(e) else 3) and (hop > 0 or way == PLUS):
            over(e, (-1 if way == PLUS else 1) * hop)

    def stage(e, n):
        if n == 0:
            arrived(sib.at[e], sib_send.at[e], sib_recv.at[e])
            rs_start(e)
            return
        if n == 1:
            rs_relay(e)
            return
        if n == 2:
            rs_end(e)
        for act in (ag_hop, ag_over):
            for way in (long_way(e), 1 - long_way(e)):
                act(e, way, n - 2)

    def stages(*todo):
        @pl.when(outer)
        def _():
            for e, n in todo:
                stage(e, n)

    def acts_over():
        for d in range(1, NZ):
            r = zrel(d) * 2 + k
            arrived(abuf.at[r], az_send.at[d], az_recv.at[d])
            remote(abuf.at[r], abuf.at[r], ax_send.at[d], ax_recv.at[d], sibling)

    def acts_product():
        loads["bi"].wait()
        for d in range(NZ):
            arrived(abuf.at[zrel(d) * 2 + 1 - k], ax_send.at[d], ax_recv.at[d])
        for lo in range(0, 16, 4):
            value = jnp.dot(abuf[lo:lo + 4].reshape(128, 512), bi[...], preferred_element_type=F32)
            apart[lo:lo + 4] = value.reshape(4, 32, 512)
        for i in range(1, 16):
            py, px = xyrel(-(i // 4), -(i % 4))
            remote(apart.at[py * 4 + px], arecv.at[i], ar_send.at[i], ar_recv.at[i], dev(y=py, x=px))

    def acts_sum():
        value = apart[col]
        for i in range(1, 16):
            arrived(arecv.at[i], ar_send.at[i], ar_recv.at[i])
            value = value + arecv[i]
        ra[col] = value.astype(BF16)
        for i in range(1, 16):
            py, px = xyrel(-(i // 4), -(i % 4))
            remote(ra.at[col], ra.at[col], aa_send.at[i], aa_recv.at[i], dev(y=py, x=px))

    def acts_end():
        for i in range(1, 16):
            py, px = xyrel(i // 4, i % 4)
            arrived(ra.at[py * 4 + px], aa_send.at[i], aa_recv.at[i])

    loads["bo"].wait()
    product(0)
    for j in (1, 5):
        far(1, j)
    for j in (2, 3, 6, 7):
        far(3, j)
    stages((0, 0))
    for j in (2, 3, 6, 7):
        garrived(1, j)
    product(1)
    for j in (0, 1, 4, 5):
        garrived(3, j)
    product(3)
    stages((0, 1), (1, 0), (3, 0))
    acts_over()
    stages((0, 2))
    for j in range(8):
        garrived(2, j)
    product(2)
    stages((1, 1), (3, 1), (0, 3), (2, 0))
    acts_product()
    stages((1, 2), (3, 2), (0, 4), (2, 1))
    stages((1, 3), (3, 3), (0, 5), (2, 2))
    stages((1, 4), (3, 4), (0, 6), (2, 3))
    acts_sum()
    stages((1, 5), (3, 5), (2, 4))
    stages((1, 6), (3, 6), (2, 5))
    stages((2, 6))
    acts_end()

    @pl.when(inner)
    def _():
        for e in (0, 1, 3, 2):
            for d in (0, 1, 7, 2, 6, 3, 5, 4):
                arrived(rg.at[block_of(e, zrel(d))], agx_send.at[e, d], agx_recv.at[e, d])
            sent(psend.at[e], sib_send.at[e], sib_recv.at[e])

    @pl.when(outer)
    def _():
        for e in range(4):
            for way in (PLUS, MINUS):
                for hop in ((0, 1, 2, 3) if way == long_way(e) else (0, 2, 3)):
                    sent(rsend.at[e, way, hop], rs_send.at[e, way, hop], rs_recv.at[e, way, hop])
                for hop in range(4 if way == long_way(e) else 3):
                    sent(rg.at[0], ag_send.at[e, way, hop], ag_recv.at[e, way, hop])
            for d in range(NZ):
                sent(rg.at[0], agx_send.at[e, d], agx_recv.at[e, d])

    gsent()
    for d in range(NZ):
        if d:
            sent(abuf.at[0], az_send.at[d], az_recv.at[d])
        sent(abuf.at[0], ax_send.at[d], ax_recv.at[d])
    for i in range(1, 16):
        sent(apart.at[0], ar_send.at[i], ar_recv.at[i])
        sent(ra.at[0], aa_send.at[i], aa_recv.at[i])


def gathered(activations, out_grads, basis_in, basis_out):
    ff, d = basis_out.shape[1], basis_in.shape[1]
    vmem, dma = pltpu.VMEM, pltpu.SemaphoreType.DMA
    any_ = pl.BlockSpec(memory_space=pltpu.HBM)
    inside = pl.BlockSpec(memory_space=pltpu.VMEM)
    return pl.pallas_call(
        comm_kernel,
        out_shape=(vmem((32, 16, ff), BF16), vmem((16, 32, d), BF16)),
        in_specs=[any_] * 4,
        out_specs=(inside, inside),
        scratch_shapes=[
            vmem((4, 128, ff), BF16), vmem((ff, ff), BF16), vmem((4, 128, ff), F32),
            vmem((4, 128, ff), BF16), vmem((4, 128, ff), BF16),
            vmem((4, 2, 4, 16, ff), BF16), vmem((4, 2, 4, 16, ff), BF16),
            vmem((16, 32, d), BF16), vmem((d, d), BF16), vmem((16, 32, d), F32), vmem((16, 32, d), F32),
            dma((5,)), dma((30,)), dma((4, 8)), dma((4,)), dma((4,)), dma((4, 2, 4)), dma((4, 2, 4)),
            dma((4, 2, 4)), dma((4, 2, 4)), dma((4, 8)), dma((4, 8)),
            dma((8,)), dma((8,)), dma((8,)), dma((8,)), dma((16,)), dma((16,)), dma((16,)), dma((16,)),
        ],
        compiler_params=pltpu.CompilerParams(
            collective_id=0, has_side_effects=True, vmem_limit_bytes=60 << 20),
        name="gather_rotate",
    )(activations, out_grads, basis_in, basis_out)


TILES = ((0, 512), (512, 1024), (1024, 1536), (1536, 1848))


def diag_kernel(lens, rg, ra, out_hbm, out, masked, sem):
    starts, total = [], 0
    for s in range(8):
        starts.append(total)
        total = total + lens[s]
    longest, begin, most = 0, 0, lens[0]
    for s in range(1, 8):
        more = lens[s] > most
        longest = jnp.where(more, s, longest)
        begin = jnp.where(more, starts[s], begin)
        most = jnp.where(more, lens[s], most)
    token = lax.broadcasted_iota(jnp.int32, (256, 1), 0)
    wraps = token < begin
    low, high = ra[0:256, :], ra[256:512, :]
    masked[0] = jnp.where(wraps, high, low)
    others = jnp.where(wraps, low, high)
    for i in range(7):
        before = i < longest
        start = jnp.where(before, starts[i], starts[i + 1])
        length = jnp.where(before, lens[i], lens[i + 1])
        start = jnp.where(start >= 256, start - 256, start)
        keep = (token >= start) & (token < start + length)
        masked[i + 1] = jnp.where(keep, others, jnp.zeros_like(others))
    copies = []
    for index, (lo, hi) in enumerate(TILES):
        low, high = rg[0:256, lo:hi], rg[256:512, lo:hi]
        long_side = jnp.where(wraps, high, low).T
        other_side = jnp.where(wraps, low, high).T
        for i in range(8):
            p = jnp.dot(long_side if i == 0 else other_side, masked[i], preferred_element_type=F32)
            if i == 0:
                out[lo:hi, :] = p * p
            elif i < 7:
                out[lo:hi, :] += p * p
            else:
                out[lo:hi, :] = (out[lo:hi, :] + p * p) * (1.0 / 512.0)
        copies.append(pltpu.make_async_copy(
            out.at[pl.ds(lo, hi - lo)], out_hbm.at[pl.ds(lo, hi - lo)], sem.at[index]))
        copies[-1].start()
    for copy in copies:
        copy.wait()


def diagonal(lens, rg, ra):
    ff, d = rg.shape[1], ra.shape[1]
    inside = pl.BlockSpec(memory_space=pltpu.VMEM)
    return pl.pallas_call(
        diag_kernel,
        out_shape=jax.ShapeDtypeStruct((ff, d), F32),
        in_specs=[pl.BlockSpec(memory_space=pltpu.SMEM), inside, inside],
        out_specs=pl.BlockSpec(memory_space=pl.ANY),
        scratch_shapes=[
            pltpu.VMEM((ff, d), F32), pltpu.VMEM((8, 256, d), BF16), pltpu.SemaphoreType.DMA((4,))],
        compiler_params=pltpu.CompilerParams(vmem_limit_bytes=48 << 20),
        name="eigen_diagonal",
    )(lens, rg, ra)


def local(activations, out_grads, basis_in, basis_out, seq_lengths):
    rg, ra = gathered(activations, out_grads, basis_in, basis_out)
    rg = rg.reshape(512, rg.shape[-1])
    ra = ra.reshape(512, ra.shape[-1])
    return diagonal(seq_lengths, rg, ra)


def solution(mesh):
    in_specs = (P("row", "col"), P("col", "row"), P("col", "row"), P("row", "col"), P())
    out_specs = P("col", "row")
    return jax.shard_map(local, mesh=mesh, in_specs=in_specs, out_specs=out_specs, check_vma=False)
```

time: 234 us -> 62.9 us (0.27)
  blocking collectives: 170 us -> 0 us
  Pallas kernels: 0 us -> 62.7 us
  between operations: 28.7 us -> 0.18 us
  matrix products: 25.6 us -> 0 us
  other arithmetic: 6.57 us -> 0 us
    psum x2 -> x0, blocking collectives: 147 us -> none  [the longest x1 74.8 us: local(): rot_acts = lax.psum(act_part, 'col').astype(jnp.bfloat16)]
    pallas_call x0 -> x2, Pallas kernels: none -> 62.7 us  [the longest x1 57 us: gathered(): pl.pallas_call(comm_kernel, out_shape=(vmem((32, 16, ff), BF16), vmem((16...]
    dot_general x10 -> x0, matrix products: 25.6 us -> none  [the longest x8 15.5 us: local(): lax.dot_general(grad_block, act_block, (((0,), (0,)), ((), ())), preferre...]
    all_gather x1 -> x0, blocking collectives: 23 us -> none  [local(): act_full = lax.all_gather(activations, 'row', axis=0, tiled=True)]
    convert_element_type x8 -> x0, other arithmetic: 5.08 us -> none  [local(): (jnp.arange(maxlen) < seq_lengths[index]).astype(jnp.bfloat16)[:, None]]
  transfers between devices with their start and end apart: 1 -> 0, of which waited for: 0 -> 0; matrix products, arithmetic and copies ran while one was open for 4% -> 0% of each run, Pallas kernels for 0% -> 0%
where the time goes in v2:
time: 62.9 us; the launch traced here: 62.8 us
  Pallas kernels  62.7 us (100%)
    pallas_call x1, Pallas kernels, gathered(): pl.pallas_call(comm_kernel, out_shape=(vmem((32, 16, ff), BF16), vmem((16...  57 us
    pallas_call x1, Pallas kernels, diagonal(): pl.pallas_call(diag_kernel, out_shape=jax.ShapeDtypeStruct((ff, d), F32),...  5.67 us

profile of v2, /device:TPU:1, one launch (start us, length us, event | category | flops | bytes accessed | tf_op | source)
XLA Modules:
  0.0 62.8 jit_solution(1730022928881990008)
XLA Ops:
  0.0 0.0 copy-start
  0.0 57.0 %gather_rotate.1 = (bf16[32,16,1848]{2,1,0:T(8,128)(2,1)S(1)}, bf16[16,32,512]{2,1,0:T(8,128)(2,1)S(1)}) custom-call(bf16[32,512]{1,0:T(8,128)(2,1)} %act.1, bf16[32,1848]{1,0:T(8,128)(2,1)} %grad.1, bf16[512,512]{1,0:T(8,128)(2,1)} %basis_in.1, bf16[1848,1848]{1,0:T(8,128)(2,1)} %basis_out.1), custom_call_target="tpu_custom_call" | custom-call | tf_op jit(solution)/shard_map/gather_rotate/pallas_call | solution.py:319
  57.0 0.0 copy-done
  57.0 5.7 %eigen_diagonal.1 = f32[1848,512]{1,0:T(8,128)} custom-call(s32[8]{0:T(128)S(1)} %copy-done, bf16[512,1848]{1,0:T(8,128)(2,1)S(1)} %bitcast.2, bf16[512,512]{1,0:T(8,128)(2,1)S(1)} %bitcast.3), custom_call_target="tpu_custom_call" | custom-call | tf_op jit(solution)/shard_map/eigen_diagonal/pallas_call | solution.py:388
Async XLA Ops:
  0.0 57.0 %copy-start = (s32[8]{0:T(128)S(1)}, s32[8]{0:T(128)}, u32[]{:S(2)}) copy-start(s32[8]{0:T(128)} %lens.1) | copy-start | bytes 100

commit v3 on v2

--- a/solution.py
+++ b/solution.py
@@ -57,8 +57,8 @@
         pl.semaphore_signal(barrier, inc=1, device_id=peer, device_id_type=MESH)
     loads = {}
     for index, (name, src, dst) in enumerate((
-            ("ga", grad.at[pl.ds(0, 16)], gbuf.at[0, pl.ds(0, 16)]),
-            ("gb", grad.at[pl.ds(16, 16)], gbuf.at[0, pl.ds(64, 16)]),
+            ("ga", grad.at[pl.ds(0, 16)], gbuf.at[pl.ds(0, 16)]),
+            ("gb", grad.at[pl.ds(16, 16)], gbuf.at[pl.ds(64, 16)]),
             ("act", act, abuf.at[row]),
             ("bi", basis_in, bi),
             ("bo", basis_out, bo))):
@@ -68,17 +68,16 @@
     pl.semaphore_wait(barrier, len(peers))
 
     def gslot(e, j):
-        return gbuf.at[e, pl.ds(16 * j, 16)]
-
-    counter = [0]
+        return gbuf.at[pl.ds(128 * e + 16 * j, 16)]
 
     def gsend(src, e, j, to):
-        remote(src, gslot(e, j), g_send.at[counter[0]], g_recv.at[e, j], to)
-        counter[0] += 1
+        remote(src, gslot(e, j), g_send.at[0], g_recv.at[e, 0 if e == 2 else j], to)
 
     def gsent():
-        for i in range(30):
-            sent(gslot(0, 0), g_send.at[i], g_recv.at[0, 0])
+        sent(gbuf.at[pl.ds(0, 480)], g_send.at[0], g_recv.at[0, 0])
+
+    def last_arrived():
+        arrived(gbuf.at[pl.ds(256, 128)], g_send.at[0], g_recv.at[2, 0])
 
     def garrived(e, j):
         arrived(gslot(e, j), g_send.at[0], g_recv.at[e, j])
@@ -99,7 +98,7 @@
 
     loads["act"].wait()
     for i, d in enumerate((1, 7, 2, 6, 3, 5, 4)):
-        remote(abuf.at[row], abuf.at[row], az_send.at[d], az_recv.at[d], dev(z=zrel(-d)))
+        remote(abuf.at[row], abuf.at[row], az_send.at[0], az_recv.at[0], dev(z=zrel(-d)))
     remote(abuf.at[row], abuf.at[row], ax_send.at[0], ax_recv.at[0], dev(k=1 - k))
 
     for d in (1, 3, 2):
@@ -122,7 +121,7 @@
 
     def product(e):
         for lo, hi in ((0, 512), (512, 1024), (1024, 1536), (1536, 1848)):
-            value = jnp.dot(gbuf[e], bo[:, lo:hi], preferred_element_type=F32)
+            value = jnp.dot(gbuf[128 * e:128 * e + 128], bo[:, lo:hi], preferred_element_type=F32)
 
             @pl.when(inner)
             def _():
@@ -134,7 +133,7 @@
 
         @pl.when(inner)
         def _():
-            remote(psend.at[e], sib.at[e], sib_send.at[e], sib_recv.at[e], sibling)
+            remote(psend.at[e], sib.at[e], sib_send.at[0], sib_recv.at[e], sibling)
 
     def own(e, j):
         at = pl.ds(pl.multiple_of(16 * j, 16), 16)
@@ -145,12 +144,12 @@
 
     def rs_send_own(e, way, index, to_owner, to):
         sign = 1 if way == PLUS else -1
-        rsend[e, way, index] = own(e, zrel(sign * to_owner)).astype(BF16)
-        remote(rsend.at[e, way, index], rrecv.at[e, way, index],
-               rs_send.at[e, way, index], rs_recv.at[e, way, index], dev(z=zrel(sign * to)))
+        rsend[8 * e + 4 * way + index] = own(e, zrel(sign * to_owner)).astype(BF16)
+        remote(rsend.at[8 * e + 4 * way + index], rrecv.at[e, way, index],
+               rs_send.at[0], rs_recv.at[e, way, index], dev(z=zrel(sign * to)))
 
     def rs_take(e, way, index):
-        arrived(rrecv.at[e, way, index], rs_send.at[e, way, index], rs_recv.at[e, way, index])
+        arrived(rrecv.at[e, way, index], rs_send.at[0], rs_recv.at[e, way, index])
         return rrecv[e, way, index].astype(F32)
 
     def rs_start(e):
@@ -160,15 +159,14 @@
         for way in (long_way(e), 1 - long_way(e)):
             rs_send_own(e, way, 2, 1, 1)
 
-    def rs_relay(e):
-        for way in (long_way(e), 1 - long_way(e)):
-            sign = 1 if way == PLUS else -1
-            value = own(e, zrel(sign * 2)) + rs_take(e, way, 0)
-            if way == long_way(e):
-                value = value + rs_take(e, way, 1)
-            rsend[e, way, 3] = value.astype(BF16)
-            remote(rsend.at[e, way, 3], rrecv.at[e, way, 3],
-                   rs_send.at[e, way, 3], rs_recv.at[e, way, 3], dev(z=zrel(sign * 2)))
+    def rs_relay(e, way):
+        sign = 1 if way == PLUS else -1
+        value = own(e, zrel(sign * 2)) + rs_take(e, way, 0)
+        if way == long_way(e):
+            value = value + rs_take(e, way, 1)
+        rsend[8 * e + 4 * way + 3] = value.astype(BF16)
+        remote(rsend.at[8 * e + 4 * way + 3], rrecv.at[e, way, 3],
+               rs_send.at[0], rs_recv.at[e, way, 3], dev(z=zrel(sign * 2)))
 
     def block_of(e, j):
         first = 2 * (((y + e) % 4) * 4 + (x + j) % 4)
@@ -184,7 +182,7 @@
 
     def over(e, d):
         at = rg.at[block_of(e, zrel(d))]
-        remote(at, at, agx_send.at[e, d % NZ], agx_recv.at[e, d % NZ], sibling)
+        remote(at, at, agx_send.at[0], agx_recv.at[e], sibling)
 
     def ag_hop(e, way, hop):
         sign = 1 if way == PLUS else -1
@@ -193,65 +191,86 @@
             return
         at = rg.at[block_of(e, zrel(-sign * hop))]
         if hop > 0:
-            arrived(at, ag_send.at[e, way, hop - 1], ag_recv.at[e, way, hop - 1])
+            arrived(at, ag_send.at[0], ag_recv.at[e, way, hop - 1])
         if hop < last:
-            remote(at, at, ag_send.at[e, way, hop], ag_recv.at[e, way, hop], dev(z=zrel(sign)))
-
-    def ag_over(e, way, hop):
-        if hop <= (4 if way == long_way(e) else 3) and (hop > 0 or way == PLUS):
-            over(e, (-1 if way == PLUS else 1) * hop)
-
-    def stage(e, n):
-        if n == 0:
-            arrived(sib.at[e], sib_send.at[e], sib_recv.at[e])
-            rs_start(e)
-            return
-        if n == 1:
-            rs_relay(e)
-            return
-        if n == 2:
-            rs_end(e)
-        for act in (ag_hop, ag_over):
-            for way in (long_way(e), 1 - long_way(e)):
-                act(e, way, n - 2)
-
-    def stages(*todo):
+            remote(at, at, ag_send.at[0], ag_recv.at[e, way, hop], dev(z=zrel(sign)))
+
+    def ag_send_block(e, way, index, d, to):
+        sign = 1 if way == PLUS else -1
+        at = rg.at[block_of(e, zrel(d))]
+        remote(at, at, ag_send.at[0], ag_recv.at[e, way, index], dev(z=zrel(sign * to)))
+
+    def ag_take(e, way, index, d):
+        at = rg.at[block_of(e, zrel(d))]
+        arrived(at, ag_send.at[0], ag_recv.at[e, way, index])
+
+    def start(e):
+        arrived(sib.at[e], sib_send.at[0], sib_recv.at[e])
+        rs_start(e)
+
+    def end(e):
+        rs_end(e)
+        ways = (long_way(e), 1 - long_way(e))
+        if e == 0:
+            for way in ways:
+                ag_hop(e, way, 0)
+        else:
+            for index in (1, 0):
+                for way in ways:
+                    ag_send_block(e, way, index, 0, index + 1)
+        over(e, 0)
+
+    def hop(e, way, n):
+        ag_hop(e, way, n)
+        over(e, (-1 if way == PLUS else 1) * n)
+
+    def forward(e, way):
+        sign = 1 if way == PLUS else -1
+        ag_take(e, way, 1, -2 * sign)
+        if way == long_way(e):
+            ag_send_block(e, way, 3, -2 * sign, 2)
+        ag_send_block(e, way, 2, -2 * sign, 1)
+        over(e, -2 * sign)
+
+    def take(e, way, n):
+        sign = 1 if way == PLUS else -1
+        ag_take(e, way, {1: 0, 3: 2, 4: 3}[n], -n * sign)
+        over(e, -n * sign)
+
+    def steps(*todo):
         @pl.when(outer)
         def _():
-            for e, n in todo:
-                stage(e, n)
+            for act, *what in todo:
+                act(*what)
 
     def acts_over():
+        arrived(abuf.at[pl.ds(0, 7)], az_send.at[0], az_recv.at[0])
         for d in range(1, NZ):
             r = zrel(d) * 2 + k
-            arrived(abuf.at[r], az_send.at[d], az_recv.at[d])
-            remote(abuf.at[r], abuf.at[r], ax_send.at[d], ax_recv.at[d], sibling)
+            remote(abuf.at[r], abuf.at[r], ax_send.at[0], ax_recv.at[0], sibling)
 
     def acts_product():
         loads["bi"].wait()
-        for d in range(NZ):
-            arrived(abuf.at[zrel(d) * 2 + 1 - k], ax_send.at[d], ax_recv.at[d])
+        arrived(abuf.at[pl.ds(0, 8)], ax_send.at[0], ax_recv.at[0])
         for lo in range(0, 16, 4):
             value = jnp.dot(abuf[lo:lo + 4].reshape(128, 512), bi[...], preferred_element_type=F32)
             apart[lo:lo + 4] = value.reshape(4, 32, 512)
         for i in range(1, 16):
             py, px = xyrel(-(i // 4), -(i % 4))
-            remote(apart.at[py * 4 + px], arecv.at[i], ar_send.at[i], ar_recv.at[i], dev(y=py, x=px))
+            remote(apart.at[py * 4 + px], arecv.at[i], ar_send.at[0], ar_recv.at[0], dev(y=py, x=px))
 
     def acts_sum():
         value = apart[col]
+        arrived(arecv.at[pl.ds(1, 15)], ar_send.at[0], ar_recv.at[0])
         for i in range(1, 16):
-            arrived(arecv.at[i], ar_send.at[i], ar_recv.at[i])
             value = value + arecv[i]
         ra[col] = value.astype(BF16)
         for i in range(1, 16):
             py, px = xyrel(-(i // 4), -(i % 4))
-            remote(ra.at[col], ra.at[col], aa_send.at[i], aa_recv.at[i], dev(y=py, x=px))
+            remote(ra.at[col], ra.at[col], aa_send.at[0], aa_recv.at[0], dev(y=py, x=px))
 
     def acts_end():
-        for i in range(1, 16):
-            py, px = xyrel(i // 4, i % 4)
-            arrived(ra.at[py * 4 + px], aa_send.at[i], aa_recv.at[i])
+        arrived(ra.at[pl.ds(0, 15)], aa_send.at[0], aa_recv.at[0])
 
     loads["bo"].wait()
     product(0)
@@ -259,56 +278,90 @@
         far(1, j)
     for j in (2, 3, 6, 7):
         far(3, j)
-    stages((0, 0))
+    steps(
+        (start, 0),
+    )
     for j in (2, 3, 6, 7):
         garrived(1, j)
     product(1)
     for j in (0, 1, 4, 5):
         garrived(3, j)
     product(3)
-    stages((0, 1), (1, 0), (3, 0))
     acts_over()
-    stages((0, 2))
-    for j in range(8):
-        garrived(2, j)
+    steps(
+        (rs_relay, 0, MINUS),
+        (rs_relay, 0, PLUS),
+        (start, 1),
+    )
+    last_arrived()
     product(2)
-    stages((1, 1), (3, 1), (0, 3), (2, 0))
+    steps(
+        (start, 3),
+        (end, 0),
+        (rs_relay, 1, MINUS),
+        (start, 2),
+        (rs_relay, 1, PLUS),
+        (rs_relay, 3, PLUS),
+        (rs_relay, 3, MINUS),
+        (hop, 0, PLUS, 1),
+        (rs_relay, 2, PLUS),
+    )
     acts_product()
-    stages((1, 2), (3, 2), (0, 4), (2, 1))
-    stages((1, 3), (3, 3), (0, 5), (2, 2))
-    stages((1, 4), (3, 4), (0, 6), (2, 3))
+    steps(
+        (hop, 0, MINUS, 1),
+        (end, 1),
+        (rs_relay, 2, MINUS),
+        (hop, 0, PLUS, 2),
+        (end, 3),
+        (hop, 0, MINUS, 2),
+        (forward, 1, PLUS),
+        (take, 1, PLUS, 1),
+        (forward, 1, MINUS),
+        (hop, 0, PLUS, 3),
+        (take, 1, MINUS, 1),
+        (end, 2),
+        (forward, 3, PLUS),
+        (take, 3, PLUS, 1),
+        (forward, 3, MINUS),
+    )
     acts_sum()
-    stages((1, 5), (3, 5), (2, 4))
-    stages((1, 6), (3, 6), (2, 5))
-    stages((2, 6))
+    steps(
+        (take, 3, MINUS, 1),
+        (hop, 0, MINUS, 3),
+        (take, 1, PLUS, 4),
+        (take, 1, PLUS, 3),
+        (take, 1, MINUS, 3),
+        (hop, 0, PLUS, 4),
+        (forward, 2, MINUS),
+        (take, 2, MINUS, 1),
+        (forward, 2, PLUS),
+        (take, 2, PLUS, 1),
+        (take, 3, PLUS, 3),
+        (take, 3, MINUS, 4),
+        (take, 3, MINUS, 3),
+        (take, 2, PLUS, 3),
+        (take, 2, MINUS, 4),
+        (take, 2, MINUS, 3),
+    )
     acts_end()
+
+    gsent()
+    sent(abuf.at[pl.ds(0, 7)], az_send.at[0], az_recv.at[0])
+    sent(abuf.at[pl.ds(0, 8)], ax_send.at[0], ax_recv.at[0])
+    sent(apart.at[pl.ds(0, 15)], ar_send.at[0], ar_recv.at[0])
+    sent(ra.at[pl.ds(0, 15)], aa_send.at[0], aa_recv.at[0])
 
     @pl.when(inner)
     def _():
+        sent(psend, sib_send.at[0], sib_recv.at[0])
         for e in (0, 1, 3, 2):
-            for d in (0, 1, 7, 2, 6, 3, 5, 4):
-                arrived(rg.at[block_of(e, zrel(d))], agx_send.at[e, d], agx_recv.at[e, d])
-            sent(psend.at[e], sib_send.at[e], sib_recv.at[e])
+            arrived(rg.at[pl.ds(8 * e, 8)], agx_send.at[0], agx_recv.at[e])
 
     @pl.when(outer)
     def _():
-        for e in range(4):
-            for way in (PLUS, MINUS):
-                for hop in ((0, 1, 2, 3) if way == long_way(e) else (0, 2, 3)):
-                    sent(rsend.at[e, way, hop], rs_send.at[e, way, hop], rs_recv.at[e, way, hop])
-                for hop in range(4 if way == long_way(e) else 3):
-                    sent(rg.at[0], ag_send.at[e, way, hop], ag_recv.at[e, way, hop])
-            for d in range(NZ):
-                sent(rg.at[0], agx_send.at[e, d], agx_recv.at[e, d])
-
-    gsent()
-    for d in range(NZ):
-        if d:
-            sent(abuf.at[0], az_send.at[d], az_recv.at[d])
-        sent(abuf.at[0], ax_send.at[d], ax_recv.at[d])
-    for i in range(1, 16):
-        sent(apart.at[0], ar_send.at[i], ar_recv.at[i])
-        sent(ra.at[0], aa_send.at[i], aa_recv.at[i])
+        sent(rsend.at[pl.ds(0, 28)], rs_send.at[0], rs_recv.at[0, 0, 0])
+        sent(rg.at[pl.ds(0, 28)], ag_send.at[0], ag_recv.at[0, 0, 0])
+        sent(rg, agx_send.at[0], agx_recv.at[0])
 
 
 def gathered(activations, out_grads, basis_in, basis_out):
@@ -322,13 +375,13 @@
         in_specs=[any_] * 4,
         out_specs=(inside, inside),
         scratch_shapes=[
-            vmem((4, 128, ff), BF16), vmem((ff, ff), BF16), vmem((4, 128, ff), F32),
+            vmem((512, ff), BF16), vmem((ff, ff), BF16), vmem((4, 128, ff), F32),
             vmem((4, 128, ff), BF16), vmem((4, 128, ff), BF16),
-            vmem((4, 2, 4, 16, ff), BF16), vmem((4, 2, 4, 16, ff), BF16),
+            vmem((32, 16, ff), BF16), vmem((4, 2, 4, 16, ff), BF16),
             vmem((16, 32, d), BF16), vmem((d, d), BF16), vmem((16, 32, d), F32), vmem((16, 32, d), F32),
-            dma((5,)), dma((30,)), dma((4, 8)), dma((4,)), dma((4,)), dma((4, 2, 4)), dma((4, 2, 4)),
-            dma((4, 2, 4)), dma((4, 2, 4)), dma((4, 8)), dma((4, 8)),
-            dma((8,)), dma((8,)), dma((8,)), dma((8,)), dma((16,)), dma((16,)), dma((16,)), dma((16,)),
+            dma((5,)), dma((1,)), dma((4, 8)), dma((1,)), dma((4,)), dma((1,)), dma((4, 2, 4)),
+            dma((1,)), dma((4, 2, 4)), dma((1,)), dma((4,)),
+            dma((1,)), dma((1,)), dma((1,)), dma((1,)), dma((1,)), dma((1,)), dma((1,)), dma((1,)),
         ],
         compiler_params=pltpu.CompilerParams(
             collective_id=0, has_side_effects=True, vmem_limit_bytes=60 << 20),

time: 62.9 us -> 58.8 us (0.935)
  Pallas kernels: 62.7 us -> 58.5 us
    pallas_call x1, Pallas kernels: 57 us -> 52.8 us  [gathered(): pl.pallas_call(comm_kernel, out_shape=(vmem((32, 16, ff), BF16), vmem((16...]
where the time goes in v3:
time: 58.8 us; the launch traced here: 58.7 us
  Pallas kernels  58.5 us (99%)
    pallas_call x1, Pallas kernels, gathered(): pl.pallas_call(comm_kernel, out_shape=(vmem((32, 16, ff), BF16), vmem((16...  52.8 us
    pallas_call x1, Pallas kernels, diagonal(): pl.pallas_call(diag_kernel, out_shape=jax.ShapeDtypeStruct((ff, d), F32),...  5.69 us

profile of v3, /device:TPU:1, one launch (start us, length us, event | category | flops | bytes accessed | tf_op | source)
XLA Modules:
  0.0 58.7 jit_solution(9492189009648993795)
XLA Ops:
  0.0 0.0 copy-start
  0.0 52.8 %gather_rotate.1 = (bf16[32,16,1848]{2,1,0:T(8,128)(2,1)S(1)}, bf16[16,32,512]{2,1,0:T(8,128)(2,1)S(1)}) custom-call(bf16[32,512]{1,0:T(8,128)(2,1)} %act.1, bf16[32,1848]{1,0:T(8,128)(2,1)} %grad.1, bf16[512,512]{1,0:T(8,128)(2,1)} %basis_in.1, bf16[1848,1848]{1,0:T(8,128)(2,1)} %basis_out.1), custom_call_target="tpu_custom_call" | custom-call | tf_op jit(solution)/shard_map/gather_rotate/pallas_call | solution.py:372
  52.8 0.0 copy-done
  52.8 5.7 %eigen_diagonal.1 = f32[1848,512]{1,0:T(8,128)} custom-call(s32[8]{0:T(128)S(1)} %copy-done, bf16[512,1848]{1,0:T(8,128)(2,1)S(1)} %bitcast.2, bf16[512,512]{1,0:T(8,128)(2,1)S(1)} %bitcast.3), custom_call_target="tpu_custom_call" | custom-call | tf_op jit(solution)/shard_map/eigen_diagonal/pallas_call | solution.py:441
Async XLA Ops:
  0.0 52.8 %copy-start = (s32[8]{0:T(128)S(1)}, s32[8]{0:T(128)}, u32[]{:S(2)}) copy-start(s32[8]{0:T(128)} %lens.1) | copy-start | bytes 100

commit v4 on v3

--- a/solution.py
+++ b/solution.py
@@ -47,6 +47,14 @@
 
     inner, outer = k == 0, k == 1
 
+    loads = {}
+
+    def load(name, src, dst):
+        loads[name] = pltpu.make_async_copy(src, dst, lsem.at[len(loads)])
+        loads[name].start()
+
+    load("ga", grad.at[pl.ds(0, 16)], gbuf.at[pl.ds(0, 16)])
+    load("gb", grad.at[pl.ds(16, 16)], gbuf.at[pl.ds(64, 16)])
     peers = [dev(z=zrel(d)) for d in range(1, NZ)]
     peers += [dev(k=1 - k)]
     for i in range(1, 16):
@@ -55,19 +63,14 @@
     barrier = pltpu.get_barrier_semaphore()
     for peer in peers:
         pl.semaphore_signal(barrier, inc=1, device_id=peer, device_id_type=MESH)
-    loads = {}
-    for index, (name, src, dst) in enumerate((
-            ("ga", grad.at[pl.ds(0, 16)], gbuf.at[pl.ds(0, 16)]),
-            ("gb", grad.at[pl.ds(16, 16)], gbuf.at[pl.ds(64, 16)]),
-            ("act", act, abuf.at[row]),
-            ("bi", basis_in, bi),
-            ("bo", basis_out, bo))):
-        loads[name] = pltpu.make_async_copy(src, dst, lsem.at[index])
-        loads[name].start()
-
+    load("act", act, abuf.at[row])
+    load("bo", basis_out, bo)
+    load("bi", basis_in, bi)
     pl.semaphore_wait(barrier, len(peers))
 
     def gslot(e, j):
+        if e in (1, 3):
+            e, j = 1 if j % 4 < 2 else 3, j % 2 + (2 if e == 3 else 0) + (4 if j >= 4 else 0)
         return gbuf.at[pl.ds(128 * e + 16 * j, 16)]
 
     def gsend(src, e, j, to):
@@ -169,8 +172,12 @@
                rs_send.at[0], rs_recv.at[e, way, 3], dev(z=zrel(sign * 2)))
 
     def block_of(e, j):
-        first = 2 * (((y + e) % 4) * 4 + (x + j) % 4)
-        second = 2 * (((y + j) % 4) * 4 + (x + e) % 4) + 1
+        if e in (1, 3):
+            other, away = j % 2 + (e - 1), jnp.where((j // 2) % 2 == 0, 1, 3)
+        else:
+            other, away = j % 4, e
+        first = 2 * (((y + away) % 4) * 4 + (x + other) % 4)
+        second = 2 * (((y + other) % 4) * 4 + (x + away) % 4) + 1
         return jnp.where(j < 4, first, second)
 
     def rs_end(e):
@@ -211,7 +218,7 @@
     def end(e):
         rs_end(e)
         ways = (long_way(e), 1 - long_way(e))
-        if e == 0:
+        if e in (0, 1):
             for way in ways:
                 ag_hop(e, way, 0)
         else:
@@ -276,70 +283,72 @@
     product(0)
     for j in (1, 5):
         far(1, j)
-    for j in (2, 3, 6, 7):
+    for j in (3, 7):
+        far(3, j)
+    for j in (0, 1, 4, 5):
+        garrived(3, j)
+    product(1)
+    for j in (2, 6):
         far(3, j)
     steps(
         (start, 0),
     )
     for j in (2, 3, 6, 7):
         garrived(1, j)
-    product(1)
-    for j in (0, 1, 4, 5):
-        garrived(3, j)
     product(3)
     acts_over()
     steps(
-        (rs_relay, 0, MINUS),
-        (rs_relay, 0, PLUS),
         (start, 1),
     )
     last_arrived()
     product(2)
     steps(
         (start, 3),
-        (end, 0),
+        (rs_relay, 0, MINUS),
+        (rs_relay, 0, PLUS),
         (rs_relay, 1, MINUS),
         (start, 2),
         (rs_relay, 1, PLUS),
         (rs_relay, 3, PLUS),
         (rs_relay, 3, MINUS),
-        (hop, 0, PLUS, 1),
         (rs_relay, 2, PLUS),
     )
     acts_product()
     steps(
-        (hop, 0, MINUS, 1),
+        (end, 0),
         (end, 1),
         (rs_relay, 2, MINUS),
+        (hop, 0, PLUS, 1),
+        (end, 3),
+        (hop, 1, PLUS, 1),
+        (hop, 0, MINUS, 1),
+        (hop, 1, MINUS, 1),
+        (end, 2),
         (hop, 0, PLUS, 2),
-        (end, 3),
-        (hop, 0, MINUS, 2),
-        (forward, 1, PLUS),
-        (take, 1, PLUS, 1),
-        (forward, 1, MINUS),
-        (hop, 0, PLUS, 3),
-        (take, 1, MINUS, 1),
-        (end, 2),
-        (forward, 3, PLUS),
-        (take, 3, PLUS, 1),
         (forward, 3, MINUS),
     )
     acts_sum()
     steps(
+        (forward, 3, PLUS),
         (take, 3, MINUS, 1),
-        (hop, 0, MINUS, 3),
-        (take, 1, PLUS, 4),
-        (take, 1, PLUS, 3),
-        (take, 1, MINUS, 3),
-        (hop, 0, PLUS, 4),
+        (take, 3, PLUS, 1),
+        (hop, 0, MINUS, 2),
+        (hop, 1, PLUS, 2),
+        (hop, 1, MINUS, 2),
+        (forward, 2, PLUS),
+        (take, 2, PLUS, 1),
         (forward, 2, MINUS),
         (take, 2, MINUS, 1),
-        (forward, 2, PLUS),
-        (take, 2, PLUS, 1),
+        (hop, 0, PLUS, 3),
         (take, 3, PLUS, 3),
+        (hop, 1, PLUS, 3),
         (take, 3, MINUS, 4),
         (take, 3, MINUS, 3),
         (take, 2, PLUS, 3),
+        (hop, 0, MINUS, 3),
+        (hop, 0, PLUS, 4),
+        (hop, 1, MINUS, 3),
+        (hop, 1, PLUS, 4),
         (take, 2, MINUS, 4),
         (take, 2, MINUS, 3),
     )

time: 58.8 us -> 58.6 us (level)
  no operation moved by 1% of the time
where the time goes in v4:
time: 58.6 us; the launch traced here: 58.3 us
  Pallas kernels  58.1 us (99%)
    pallas_call x1, Pallas kernels, gathered(): pl.pallas_call(comm_kernel, out_shape=(vmem((32, 16, ff), BF16), vmem((16...  52.5 us
    pallas_call x1, Pallas kernels, diagonal(): pl.pallas_call(diag_kernel, out_shape=jax.ShapeDtypeStruct((ff, d), F32),...  5.67 us

profile of v4, /device:TPU:1, one launch (start us, length us, event | category | flops | bytes accessed | tf_op | source)
XLA Modules:
  0.0 58.3 jit_solution(17211744157735553993)
XLA Ops:
  0.0 0.0 copy-start
  0.0 52.5 %gather_rotate.1 = (bf16[32,16,1848]{2,1,0:T(8,128)(2,1)S(1)}, bf16[16,32,512]{2,1,0:T(8,128)(2,1)S(1)}) custom-call(bf16[32,512]{1,0:T(8,128)(2,1)} %act.1, bf16[32,1848]{1,0:T(8,128)(2,1)} %grad.1, bf16[512,512]{1,0:T(8,128)(2,1)} %basis_in.1, bf16[1848,1848]{1,0:T(8,128)(2,1)} %basis_out.1), custom_call_target="tpu_custom_call" | custom-call | tf_op jit(solution)/shard_map/gather_rotate/pallas_call | solution.py:381
  52.5 0.0 copy-done
  52.5 5.7 %eigen_diagonal.1 = f32[1848,512]{1,0:T(8,128)} custom-call(s32[8]{0:T(128)S(1)} %copy-done, bf16[512,1848]{1,0:T(8,128)(2,1)S(1)} %bitcast.2, bf16[512,512]{1,0:T(8,128)(2,1)S(1)} %bitcast.3), custom_call_target="tpu_custom_call" | custom-call | tf_op jit(solution)/shard_map/eigen_diagonal/pallas_call | solution.py:450
Async XLA Ops:
  0.0 52.5 %copy-start = (s32[8]{0:T(128)S(1)}, s32[8]{0:T(128)}, u32[]{:S(2)}) copy-start(s32[8]{0:T(128)} %lens.1) | copy-start | bytes 100
